TPU v7x, 32 devices: a whole 2x2x4 slice. The times are simulated.
32 devices in a mesh: groups: 2 (over x), frame: 16 (over z, y, core).
Axes of the slice: x: 2, y: 2, z: 4, core: 2. Of those that a mesh axis runs over, the one named last changes fastest.
Arguments:
- query_rows: bfloat16 [8192, 2560], P(('groups', 'frame')), parts along dimension 0, may hold values from -60 to 60
- key_rows: bfloat16 [8192, 2560], P(('groups', 'frame')), parts along dimension 0, may hold values from -4 to 4
- value_rows: bfloat16 [8192, 2560], P(('groups', 'frame')), parts along dimension 0, may hold values from -6 to 6
- tile_mask: int32 [128, 27], P(('groups', 'frame')), parts along dimension 0, may hold values from 0 to 1, as said below
- head_weight: bfloat16 [2560, 64], replicated, may hold values from -0.125 to 0.125
- latent: float32 [8192, 64], P(('groups', 'frame')), parts along dimension 0, may hold values from -6 to 6
- step_index: int32 [2], P('groups'), parts along dimension 0, may hold values from 0 to 24
Outputs:
- guided: float32 [8192, 64], P(('groups', 'frame')), parts along dimension 0
- clean: float32 [8192, 64], P(('groups', 'frame')), parts along dimension 0
- latent_next: float32 [8192, 64], P(('groups', 'frame')), parts along dimension 0
There are 2 independent parts, one for each index of `groups`. A program takes and returns all parts, laid end to end along the dimension named above; an argument that names none is the same for every part. Nothing has to cross between parts.
Inputs may be any that keep to these rules, and one draw needn't show every extreme that they name: `tile_mask`: entries are 0 or 1; entry 13 (the query tile itself) is always 1.
All inputs are finite; a program needn't handle non-finite values.
Results may differ from a plain program's by a relative error of at most 0.0041.
Values may be sent and summed in bfloat16 or wider, within the bound.
A program may use at most 128 MiB of HBM per device.

v0:
```python
import math

import jax
import jax.numpy as jnp
from jax import lax
from jax.sharding import PartitionSpec as P

HEADS = 20
HD = 128
SH = 4
SW = 8
SAMPLE_STEPS = 50


GUIDANCE = 5.0
FLOW_SHIFT = 5.0


def passed_along(value, axis, steps):
    count = lax.axis_size(axis)
    pairs = [(source, (source + steps) % count) for source in range(count)]
    return lax.ppermute(value, axis, pairs)


def flow_sigma(moment):
    remain = 1.0 - moment / SAMPLE_STEPS
    return FLOW_SHIFT * remain / (1.0 + (FLOW_SHIFT - 1.0) * remain)


def edge_range(offset):
    if offset < 0:
        return (1, 2)
    if offset > 0:
        return (0, 1)
    return (0, 2)


def direct_window(stacked, block_count, block_cols):
    received_parts = {}
    for frame_step in (1, 0, -1):
        for row_step in (1, 0, -1):
            for col_step in (1, 0, -1):
                distance = frame_step * block_count + row_step * block_cols + col_step
                row_start, row_stop = edge_range(row_step)
                col_start, col_stop = edge_range(col_step)
                outgoing = stacked[row_start:row_stop, col_start:col_stop]
                if frame_step == 0 and row_step == 0 and (col_step == 0):
                    received = outgoing
                elif row_step == 0 and col_step == 0:
                    received = passed_along(outgoing, "frame", -distance)
                elif row_step != 0 and col_step != 0:
                    received = passed_along(outgoing, "frame", -distance)
                else:
                    received = passed_along(outgoing, "frame", -distance)
                received_parts[frame_step, row_step, col_step] = received
    planes = []
    for frame_step in (-1, 0, 1):
        row_parts = []
        for row_step in (-1, 0, 1):
            col_parts = [received_parts[frame_step, row_step, col_step] for col_step in (-1, 0, 1)]
            row_parts.append(jnp.concatenate(col_parts, axis=1))
        planes.append(jnp.concatenate(row_parts, axis=0))
    return planes


def window_allowed(tile_mask, frame_tile, block_row, block_col, tile_frames):
    offsets = jnp.arange(27, dtype=jnp.int32)
    frame_step = offsets // 9 - 1
    row_step = offsets // 3 % 3 - 1
    col_step = offsets % 3 - 1
    local_tile = jnp.arange(4, dtype=jnp.int32)
    tile_row = 2 * block_row + local_tile // 2
    tile_col = 2 * block_col + local_tile % 2
    frame_there = frame_tile + frame_step
    row_there = tile_row[:, None] + row_step[None, :]
    col_there = tile_col[:, None] + col_step[None, :]
    usable = ((frame_there >= 0) & (frame_there < tile_frames))[None, :]
    usable = usable & (row_there >= 0) & (row_there < SH) & (col_there >= 0) & (col_there < SW)
    return usable & (tile_mask > 0)


def attend_window(query_rows, planes, allowed):
    tok_rows, inner_width = query_rows.shape
    tile_tok = tok_rows // 4
    query_tiles = query_rows.reshape(4, tile_tok, inner_width)
    mask_full = allowed[:, None, :, None]

    def one_head(head_number, result_rows):
        key_planes = [lax.dynamic_slice_in_dim(plane, head_number * HD, HD, 3) for plane in planes]
        value_planes = [
            lax.dynamic_slice_in_dim(plane, inner_width + head_number * HD, HD, 3)
            for plane in planes
        ]
        key_list = []
        value_list = []
        for row_local in range(2):
            for col_local in range(2):
                key_list.append(
                    jnp.stack(
                        [
                            part[row_local : row_local + 3, col_local : col_local + 3]
                            for part in key_planes
                        ]
                    ).reshape(27 * tile_tok, HD)
                )
                value_list.append(
                    jnp.stack(
                        [
                            part[row_local : row_local + 3, col_local : col_local + 3]
                            for part in value_planes
                        ]
                    ).reshape(27 * tile_tok, HD)
                )
        key_tiles = jnp.stack(key_list)
        value_tiles = jnp.stack(value_list)
        head_query = lax.dynamic_slice_in_dim(query_tiles, head_number * HD, HD, 2)
        scores = jnp.einsum(
            "qtd,qkd->qtk", head_query, key_tiles, preferred_element_type=jnp.float32
        ) / math.sqrt(HD)
        scores = scores.reshape(4, tile_tok, 27, tile_tok)
        scores = jnp.where(mask_full, scores, -1e30)
        row_max = jnp.max(scores, axis=(2, 3), keepdims=True)
        shifted = jnp.where(mask_full, jnp.exp(scores - row_max), 0.0)
        weights = (shifted / jnp.sum(shifted, axis=(2, 3), keepdims=True)).astype(jnp.bfloat16)
        weights = weights.reshape(4, tile_tok, 27 * tile_tok)
        head_out = jnp.einsum(
            "qtk,qkd->qtd", weights, value_tiles, preferred_element_type=jnp.float32
        ).astype(jnp.bfloat16)
        return lax.dynamic_update_slice_in_dim(result_rows, head_out, head_number * HD, 2)

    result_rows = lax.fori_loop(
        0, HEADS, one_head, jnp.zeros((4, tile_tok, inner_width), jnp.bfloat16)
    )
    return result_rows.reshape(tok_rows, inner_width)


def per_device(query_rows, key_rows, value_rows, tile_mask, head_weight, latent, step_index):
    frame_count = lax.axis_size("frame")
    frame_index = lax.axis_index("frame")
    half_size = frame_count // 2
    block_cols = SW // 2
    block_count = SH // 2 * block_cols
    tile_frames = frame_count // (2 * block_count)
    frame_tile = frame_index // block_count % tile_frames
    block_spot = frame_index % block_count
    block_row = block_spot // block_cols
    block_col = block_spot % block_cols
    tok_rows, inner_width = query_rows.shape
    tile_tok = tok_rows // 4
    stacked = jnp.concatenate([key_rows, value_rows], axis=1).reshape(
        2, 2, tile_tok, 2 * inner_width
    )
    planes = direct_window(stacked, block_count, block_cols)
    allowed = window_allowed(tile_mask, frame_tile, block_row, block_col, tile_frames)
    attention = attend_window(query_rows, planes, allowed)
    velocity = jnp.dot(attention, head_weight, preferred_element_type=jnp.float32)
    partner_rows = passed_along(velocity, "frame", half_size)
    is_cond = frame_index < half_size
    cond_rows = jnp.where(is_cond, velocity, partner_rows)
    uncond_rows = jnp.where(is_cond, partner_rows, velocity)
    guided = uncond_rows + GUIDANCE * (cond_rows - uncond_rows)
    moment = step_index[0].astype(jnp.float32)
    sigma_now = flow_sigma(moment)
    step_size = flow_sigma(moment + 1.0) - sigma_now
    clean = latent - sigma_now * guided
    latent_next = latent + step_size * guided
    return (guided, clean, latent_next)


def solution(mesh):
    placed = (
        P(("groups", "frame"), None),
        P(("groups", "frame"), None),
        P(("groups", "frame"), None),
        P(("groups", "frame"), None),
        P(),
        P(("groups", "frame"), None),
        P("groups"),
    )
    return jax.shard_map(
        per_device,
        mesh=mesh,
        in_specs=placed,
        out_specs=(
            P(("groups", "frame"), None),
            P(("groups", "frame"), None),
            P(("groups", "frame"), None),
        ),
        check_vma=False,
    )
```

profile of v0, /device:TPU:0, one launch (start us, length us, event | category | flops | bytes accessed | tf_op | source)
XLA Modules:
  0.0 654.3 jit_solution(14808526750160094436)
XLA Ops:
  3.6 2.5 collective-permute-start.9
  6.1 3.5 collective-permute-start
  9.9 3.2 collective-permute-start.14
  13.1 1.8 fusion.45
  14.9 38.1 %collective-permute-done.11 = bf16[1,1,64,5120]{3,2,1,0:T(8,128)(2,1)S(1)} collective-permute-done((bf16[1,1,64,5120]{3,2,1,0:T(8,128)(2,1)S(1)}, bf16[1,1,64,5120]{3,2,1,0:T(8,128)(2,1)S(1)}, u32[]{:S(2)}, u32[]{:S(2)}) %collective-permute-start.11) | collective-permute-done | bytes 655392 | tf_op jit(solution)/shard_map/ppermute | solution.py:22
  53.0 26.6 %collective-permute-start.6 = (bf16[1,1,64,5120]{3,2,1,0:T(8,128)(2,1)S(1)}, bf16[1,1,64,5120]{3,2,1,0:T(8,128)(2,1)}, u32[]{:S(2)}, u32[]{:S(2)}) collective-permute-start(bf16[1,1,64,5120]{3,2,1,0:T(8,128)(2,1)S(1)} %get-tuple-element.228), channel_id=1, source_target_pairs={{0,5},{1,6},{2,7},{3,8},{4,9},{5,10},{6,11},{7,12},{8,13},{9,14},{... | collective-permute-start | bytes 1966088 | tf_op jit(solution)/shard_map/ppermute | solution.py:22
  79.6 1.7 fusion.44
  81.3 24.6 %collective-permute-done.16 = bf16[1,1,64,5120]{3,2,1,0:T(8,128)(2,1)S(1)} collective-permute-done((bf16[1,1,64,5120]{3,2,1,0:T(8,128)(2,1)}, bf16[1,1,64,5120]{3,2,1,0:T(8,128)(2,1)S(1)}, u32[]{:S(2)}, u32[]{:S(2)}) %collective-permute-start.16) | collective-permute-done | bytes 655392 | tf_op jit(solution)/shard_map/ppermute | solution.py:22
  106.8 3.2 collective-permute-start.12
  110.0 8.1 %collective-permute-start.13 = (bf16[2,1,64,5120]{3,2,1,0:T(8,128)(2,1)}, bf16[2,1,64,5120]{3,2,1,0:T(8,128)(2,1)}, u32[]{:S(2)}, u32[]{:S(2)}) collective-permute-start(bf16[2,1,64,5120]{3,2,1,0:T(8,128)(2,1)} %get-tuple-element.233), channel_id=1, source_target_pairs={{0,15},{1,0},{2,1},{3,2},{4,3},{5,4},{6,5},{7,6},{8,7},{9,8},{10,9... | collective-permute-start | bytes 3932168 | tf_op jit(solution)/shard_map/ppermute | solution.py:22
  118.2 2.9 collective-permute-start.10
  123.4 61.4 %collective-permute-done.8 = bf16[1,1,64,5120]{3,2,1,0:T(8,128)(2,1)} collective-permute-done((bf16[1,1,64,5120]{3,2,1,0:T(8,128)(2,1)}, bf16[1,1,64,5120]{3,2,1,0:T(8,128)(2,1)}, u32[]{:S(2)}, u32[]{:S(2)}) %collective-permute-start.8) | collective-permute-done | bytes 655392 | tf_op jit(solution)/shard_map/ppermute | solution.py:22
  184.8 5.8 collective-permute-start.4
  190.7 7.0 %collective-permute-start.3 = (bf16[2,1,64,5120]{3,2,1,0:T(8,128)(2,1)}, bf16[2,1,64,5120]{3,2,1,0:T(8,128)(2,1)S(1)}, u32[]{:S(2)}, u32[]{:S(2)}) collective-permute-start(bf16[2,1,64,5120]{3,2,1,0:T(8,128)(2,1)} %get-tuple-element.232), channel_id=1, source_target_pairs={{0,9},{1,10},{2,11},{3,12},{4,13},{5,14},{6,15},{7,0},{8,1},{9,2},... | collective-permute-start | bytes 3932168 | tf_op jit(solution)/shard_map/ppermute | solution.py:22
  197.8 6.1 collective-permute-start.5
  203.9 4.4 collective-permute-start.1
  208.3 8.8 %maximum_maximum_fusion.1 = bf16[4,4,64,5120]{3,2,1,0:T(8,128)(2,1)} fusion(bf16[1,1,64,5120]{3,2,1,0:T(8,128)(2,1)} %copy-done.4, bf16[1,2,64,5120]{3,2,1,0:T(8,128)(2,1)} %collective-permute-done.15, bf16[1,1,64,5120]{3,2,1,0:T(8,128)(2,1)} %copy-done.3, bf16[2,1,64,5120]{3,2,1,0:T(8,128)(2,1)} %collective-permute-done.13, ...), kind=kLoop, calls=%fused_computation.53 | loop fusion | flops 41943040 | bytes 20971520 | tf_op jit(solution)/shard_map/concatenate | solution.py:62
  217.1 63.8 %collective-permute-done.3 = bf16[2,1,64,5120]{3,2,1,0:T(8,128)(2,1)S(1)} collective-permute-done((bf16[2,1,64,5120]{3,2,1,0:T(8,128)(2,1)}, bf16[2,1,64,5120]{3,2,1,0:T(8,128)(2,1)S(1)}, u32[]{:S(2)}, u32[]{:S(2)}) %collective-permute-start.3) | collective-permute-done | bytes 1310752 | tf_op jit(solution)/shard_map/ppermute | solution.py:22
  280.9 167.0 %collective-permute-done.5 = bf16[2,1,64,5120]{3,2,1,0:T(8,128)(2,1)S(1)} collective-permute-done((bf16[2,1,64,5120]{3,2,1,0:T(8,128)(2,1)}, bf16[2,1,64,5120]{3,2,1,0:T(8,128)(2,1)S(1)}, u32[]{:S(2)}, u32[]{:S(2)}) %collective-permute-start.5) | collective-permute-done | bytes 1310752 | tf_op jit(solution)/shard_map/ppermute | solution.py:22
  447.9 7.9 %maximum_maximum_fusion = bf16[4,4,64,5120]{3,2,1,0:T(8,128)(2,1)} fusion(bf16[1,1,64,5120]{3,2,1,0:T(8,128)(2,1)} %collective-permute-done.8, bf16[1,2,64,5120]{3,2,1,0:T(8,128)(2,1)S(1)} %collective-permute-done.7, bf16[1,1,64,5120]{3,2,1,0:T(8,128)(2,1)} %collective-permute-done.6, bf16[2,1,64,5120]{3,2,1,0:T(8,128)(2,1)S(1)} %collective-permute-done.5, ...), kind=kLoop, calls=%fused_computation.52 | loop fusion | flops 41943040 | bytes 20971520 | tf_op jit(solution)/shard_map/concatenate | solution.py:62
  456.9 172.1 %while.15 = (s32[]{:T(128)}, bf16[4,64,2560]{2,1,0:T(8,128)(2,1)}, pred[4,1,27,1]{2,0,3,1:T(4,128)(4,1)S(1)}, bf16[4,64,2560]{2,1,0:T(8,128)(2,1)}, bf16[4,4,64,...) while((s32[]{:T(128)}, bf16[4,64,2560]{2,1,0:T(8,128)(2,1)}, ...), condition=%wide.region_3.4_spmd, body=%wide.region_0.3_spmd.sunk | while | flops 238470848 | bytes 24941196 | solution.py:131
  456.9 2.4 dynamic-slice_bitcast_fusion.17
  459.7 3.1 fusion.61
  465.5 2.4 dynamic-slice_bitcast_fusion.17
  468.3 3.1 fusion.61
  474.1 2.6 dynamic-slice_bitcast_fusion.17
  477.1 3.1 fusion.61
  482.9 2.3 dynamic-slice_bitcast_fusion.17
  485.5 3.1 fusion.61
  491.4 2.3 dynamic-slice_bitcast_fusion.17
  494.1 3.1 fusion.61
  499.9 2.4 dynamic-slice_bitcast_fusion.17
  502.7 3.1 fusion.61
  508.5 2.5 dynamic-slice_bitcast_fusion.17
  511.4 3.1 fusion.61
  517.2 2.4 dynamic-slice_bitcast_fusion.17
  520.0 3.1 fusion.61
  525.8 2.3 dynamic-slice_bitcast_fusion.17
  528.5 3.1 fusion.61
  534.4 2.3 dynamic-slice_bitcast_fusion.17
  537.1 3.1 fusion.61
  542.9 2.5 dynamic-slice_bitcast_fusion.17
  545.8 3.1 fusion.61
  551.6 2.3 dynamic-slice_bitcast_fusion.17
  554.3 3.1 fusion.61
  560.1 2.3 dynamic-slice_bitcast_fusion.17
  562.8 3.1 fusion.61
  568.6 2.7 dynamic-slice_bitcast_fusion.17
  571.7 3.1 fusion.61
  577.5 2.5 dynamic-slice_bitcast_fusion.17
  580.4 3.1 fusion.61
  586.3 2.3 dynamic-slice_bitcast_fusion.17
  589.0 3.1 fusion.61
  594.8 2.3 dynamic-slice_bitcast_fusion.17
  597.5 3.1 fusion.61
  603.3 2.4 dynamic-slice_bitcast_fusion.17
  606.1 3.1 fusion.61
  611.9 2.3 dynamic-slice_bitcast_fusion.17
  614.6 3.1 fusion.61
  620.4 2.4 dynamic-slice_bitcast_fusion.17
  623.2 3.1 fusion.61
  629.0 1.8 fusion.50
  630.9 18.4 %collective-permute-start.17 = (f32[256,64]{0,1:T(8,128)S(1)}, f32[256,64]{0,1:T(8,128)S(1)}, u32[]{:S(2)}, u32[]{:S(2)}) collective-permute-start(f32[256,64]{0,1:T(8,128)S(1)} %fusion.50), channel_id=1, source_target_pairs={{0,8},{1,9},{2,10},{3,11},{4,12},{5,13},{6,14},{7,15},{8,0},{9,1},... | collective-permute-start | bytes 196616 | tf_op jit(solution)/shard_map/ppermute | solution.py:22
  650.0 3.0 collective-permute-done.17
  (304 shorter events, 69.4 us)
Async XLA Ops:
  0.6 628.4 %copy-start = (bf16[2560,64]{0,1:T(8,128)(2,1)S(1)}, bf16[2560,64]{0,1:T(8,128)(2,1)}, u32[]{:S(2)}) copy-start(bf16[2560,64]{0,1:T(8,128)(2,1)} %param.13) | copy-start | bytes 983044
  0.6 1.8 copy-start.1
  3.6 106.4 %collective-permute-start.9 = (bf16[1,1,64,5120]{3,2,1,0:T(8,128)(2,1)S(1)}, bf16[1,1,64,5120]{3,2,1,0:T(8,128)(2,1)}, u32[]{:S(2)}, u32[]{:S(2)}) collective-permute-start(bf16[1,1,64,5120]{3,2,1,0:T(8,128)(2,1)S(1)} %get-tuple-element.226), channel_id=1, source_target_pairs={{0,5},{1,6},{2,7},{3,8},{4,9},{5,10},{6,11},{7,12},{8,13},{9,14},{... | collective-permute-start | bytes 1966088 | tf_op jit(solution)/shard_map/ppermute | solution.py:22
  6.1 112.1 %collective-permute-start = (bf16[1,1,64,5120]{3,2,1,0:T(8,128)(2,1)S(1)}, bf16[1,1,64,5120]{3,2,1,0:T(8,128)(2,1)}, u32[]{:S(2)}, u32[]{:S(2)}) collective-permute-start(bf16[1,1,64,5120]{3,2,1,0:T(8,128)(2,1)S(1)} %get-tuple-element.226), channel_id=1, source_target_pairs={{0,13},{1,14},{2,15},{3,0},{4,1},{5,2},{6,3},{7,4},{8,5},{9,6},{10... | collective-permute-start | bytes 1966088 | tf_op jit(solution)/shard_map/ppermute | solution.py:22
  9.6 43.4 %collective-permute-start.11 = (bf16[1,1,64,5120]{3,2,1,0:T(8,128)(2,1)S(1)}, bf16[1,1,64,5120]{3,2,1,0:T(8,128)(2,1)S(1)}, u32[]{:S(2)}, u32[]{:S(2)}) collective-permute-start(bf16[1,1,64,5120]{3,2,1,0:T(8,128)(2,1)S(1)} %get-tuple-element.229), channel_id=1, source_target_pairs={{0,3},{1,4},{2,5},{3,6},{4,7},{5,8},{6,9},{7,10},{8,11},{9,12},{10... | collective-permute-start | bytes 1966088 | tf_op jit(solution)/shard_map/ppermute | solution.py:22
  9.6 111.5 %collective-permute-start.2 = (bf16[1,1,64,5120]{3,2,1,0:T(8,128)(2,1)S(1)}, bf16[1,1,64,5120]{3,2,1,0:T(8,128)(2,1)}, u32[]{:S(2)}, u32[]{:S(2)}) collective-permute-start(bf16[1,1,64,5120]{3,2,1,0:T(8,128)(2,1)S(1)} %get-tuple-element.229), channel_id=1, source_target_pairs={{0,11},{1,12},{2,13},{3,14},{4,15},{5,0},{6,1},{7,2},{8,3},{9,4},{... | collective-permute-start | bytes 1966088 | tf_op jit(solution)/shard_map/ppermute | solution.py:22
  9.9 69.7 %collective-permute-start.14 = (bf16[1,1,64,5120]{3,2,1,0:T(8,128)(2,1)S(1)}, bf16[1,1,64,5120]{3,2,1,0:T(8,128)(2,1)S(1)}, u32[]{:S(2)}, u32[]{:S(2)}) collective-permute-start(bf16[1,1,64,5120]{3,2,1,0:T(8,128)(2,1)S(1)} %get-tuple-element.228), channel_id=1, source_target_pairs={{0,13},{1,14},{2,15},{3,0},{4,1},{5,2},{6,3},{7,4},{8,5},{9,6},{10... | collective-permute-start | bytes 1966088 | tf_op jit(solution)/shard_map/ppermute | solution.py:22
  53.0 28.4 %copy-start.2 = (bf16[1,1,64,5120]{3,2,1,0:T(8,128)(2,1)}, bf16[1,1,64,5120]{3,2,1,0:T(8,128)(2,1)S(1)}, u32[]{:S(2)}) copy-start(bf16[1,1,64,5120]{3,2,1,0:T(8,128)(2,1)S(1)} %collective-permute-done.11) | copy-start | bytes 1966084
  53.0 69.0 %collective-permute-start.6 = (bf16[1,1,64,5120]{3,2,1,0:T(8,128)(2,1)S(1)}, bf16[1,1,64,5120]{3,2,1,0:T(8,128)(2,1)}, u32[]{:S(2)}, u32[]{:S(2)}) collective-permute-start(bf16[1,1,64,5120]{3,2,1,0:T(8,128)(2,1)S(1)} %get-tuple-element.228), channel_id=1, source_target_pairs={{0,5},{1,6},{2,7},{3,8},{4,9},{5,10},{6,11},{7,12},{8,13},{9,14},{... | collective-permute-start | bytes 1966088 | tf_op jit(solution)/shard_map/ppermute | solution.py:22
  79.6 1.7 copy-start.3
  79.6 111.0 %copy-start.7 = (s32[4,27]{1,0:T(4,128)S(1)}, s32[4,27]{1,0:T(4,128)}, u32[]{:S(2)}) copy-start(s32[4,27]{1,0:T(4,128)} %param.12) | copy-start | bytes 1300
  79.6 26.4 %collective-permute-start.16 = (bf16[1,1,64,5120]{3,2,1,0:T(8,128)(2,1)}, bf16[1,1,64,5120]{3,2,1,0:T(8,128)(2,1)S(1)}, u32[]{:S(2)}, u32[]{:S(2)}) collective-permute-start(bf16[1,1,64,5120]{3,2,1,0:T(8,128)(2,1)} %get-tuple-element.227), channel_id=1, source_target_pairs={{0,11},{1,12},{2,13},{3,14},{4,15},{5,0},{6,1},{7,2},{8,3},{9,4},{... | collective-permute-start | bytes 1966088 | tf_op jit(solution)/shard_map/ppermute | solution.py:22
  106.0 0.8 copy-start.4
  106.8 83.9 %collective-permute-start.12 = (bf16[2,1,64,5120]{3,2,1,0:T(8,128)(2,1)}, bf16[2,1,64,5120]{3,2,1,0:T(8,128)(2,1)}, u32[]{:S(2)}, u32[]{:S(2)}) collective-permute-start(bf16[2,1,64,5120]{3,2,1,0:T(8,128)(2,1)} %get-tuple-element.232), channel_id=1, source_target_pairs={{0,1},{1,2},{2,3},{3,4},{4,5},{5,6},{6,7},{7,8},{8,9},{9,10},{10,1... | collective-permute-start | bytes 3932168 | tf_op jit(solution)/shard_map/ppermute | solution.py:22
  110.0 87.8 %collective-permute-start.13 = (bf16[2,1,64,5120]{3,2,1,0:T(8,128)(2,1)}, bf16[2,1,64,5120]{3,2,1,0:T(8,128)(2,1)}, u32[]{:S(2)}, u32[]{:S(2)}) collective-permute-start(bf16[2,1,64,5120]{3,2,1,0:T(8,128)(2,1)} %get-tuple-element.233), channel_id=1, source_target_pairs={{0,15},{1,0},{2,1},{3,2},{4,3},{5,4},{6,5},{7,6},{8,7},{9,8},{10,9... | collective-permute-start | bytes 3932168 | tf_op jit(solution)/shard_map/ppermute | solution.py:22
  118.2 85.7 %collective-permute-start.10 = (bf16[1,2,64,5120]{3,2,1,0:T(8,128)(2,1)}, bf16[1,2,64,5120]{3,2,1,0:T(8,128)(2,1)}, u32[]{:S(2)}, u32[]{:S(2)}) collective-permute-start(bf16[1,2,64,5120]{3,2,1,0:T(8,128)(2,1)} %bitcast.28), channel_id=1, source_target_pairs={{0,4},{1,5},{2,6},{3,7},{4,8},{5,9},{6,10},{7,11},{8,12},{9,13},{1... | collective-permute-start | bytes 3932168 | tf_op jit(solution)/shard_map/ppermute | solution.py:22
  121.1 87.2 %collective-permute-start.15 = (bf16[1,2,64,5120]{3,2,1,0:T(8,128)(2,1)}, bf16[1,2,64,5120]{3,2,1,0:T(8,128)(2,1)}, u32[]{:S(2)}, u32[]{:S(2)}) collective-permute-start(bf16[1,2,64,5120]{3,2,1,0:T(8,128)(2,1)} %bitcast.29), channel_id=1, source_target_pairs={{0,12},{1,13},{2,14},{3,15},{4,0},{5,1},{6,2},{7,3},{8,4},{9,5},{1... | collective-permute-start | bytes 3932168 | tf_op jit(solution)/shard_map/ppermute | solution.py:22
  122.0 62.8 %collective-permute-start.8 = (bf16[1,1,64,5120]{3,2,1,0:T(8,128)(2,1)}, bf16[1,1,64,5120]{3,2,1,0:T(8,128)(2,1)}, u32[]{:S(2)}, u32[]{:S(2)}) collective-permute-start(bf16[1,1,64,5120]{3,2,1,0:T(8,128)(2,1)} %get-tuple-element.227), channel_id=1, source_target_pairs={{0,3},{1,4},{2,5},{3,6},{4,7},{5,8},{6,9},{7,10},{8,11},{9,12},{10... | collective-permute-start | bytes 1966088 | tf_op jit(solution)/shard_map/ppermute | solution.py:22
  184.8 263.1 %collective-permute-start.4 = (bf16[2,2,64,5120]{3,2,1,0:T(8,128)(2,1)S(1)}, bf16[2,2,64,5120]{3,2,1,0:T(8,128)(2,1)S(1)}, u32[]{:S(2)}, u32[]{:S(2)}) collective-permute-start(bf16[2,2,64,5120]{3,2,1,0:T(8,128)(2,1)S(1)} %bitcast.74), channel_id=1, source_target_pairs={{0,8},{1,9},{2,10},{3,11},{4,12},{5,13},{6,14},{7,15},{8,0},{9,1},... | collective-permute-start | bytes 7864328 | tf_op jit(solution)/shard_map/ppermute | solution.py:22
  190.7 90.1 %collective-permute-start.3 = (bf16[2,1,64,5120]{3,2,1,0:T(8,128)(2,1)}, bf16[2,1,64,5120]{3,2,1,0:T(8,128)(2,1)S(1)}, u32[]{:S(2)}, u32[]{:S(2)}) collective-permute-start(bf16[2,1,64,5120]{3,2,1,0:T(8,128)(2,1)} %get-tuple-element.232), channel_id=1, source_target_pairs={{0,9},{1,10},{2,11},{3,12},{4,13},{5,14},{6,15},{7,0},{8,1},{9,2},... | collective-permute-start | bytes 3932168 | tf_op jit(solution)/shard_map/ppermute | solution.py:22
  197.8 250.1 %collective-permute-start.5 = (bf16[2,1,64,5120]{3,2,1,0:T(8,128)(2,1)}, bf16[2,1,64,5120]{3,2,1,0:T(8,128)(2,1)S(1)}, u32[]{:S(2)}, u32[]{:S(2)}) collective-permute-start(bf16[2,1,64,5120]{3,2,1,0:T(8,128)(2,1)} %get-tuple-element.233), channel_id=1, source_target_pairs={{0,7},{1,8},{2,9},{3,10},{4,11},{5,12},{6,13},{7,14},{8,15},{9,0},... | collective-permute-start | bytes 3932168 | tf_op jit(solution)/shard_map/ppermute | solution.py:22
  203.9 244.0 %collective-permute-start.1 = (bf16[1,2,64,5120]{3,2,1,0:T(8,128)(2,1)}, bf16[1,2,64,5120]{3,2,1,0:T(8,128)(2,1)S(1)}, u32[]{:S(2)}, u32[]{:S(2)}) collective-permute-start(bf16[1,2,64,5120]{3,2,1,0:T(8,128)(2,1)} %bitcast.28), channel_id=1, source_target_pairs={{0,12},{1,13},{2,14},{3,15},{4,0},{5,1},{6,2},{7,3},{8,4},{9,5},{1... | collective-permute-start | bytes 3932168 | tf_op jit(solution)/shard_map/ppermute | solution.py:22
  208.3 239.6 %collective-permute-start.7 = (bf16[1,2,64,5120]{3,2,1,0:T(8,128)(2,1)}, bf16[1,2,64,5120]{3,2,1,0:T(8,128)(2,1)S(1)}, u32[]{:S(2)}, u32[]{:S(2)}) collective-permute-start(bf16[1,2,64,5120]{3,2,1,0:T(8,128)(2,1)} %bitcast.29), channel_id=1, source_target_pairs={{0,4},{1,5},{2,6},{3,7},{4,8},{5,9},{6,10},{7,11},{8,12},{9,13},{1... | collective-permute-start | bytes 3932168 | tf_op jit(solution)/shard_map/ppermute | solution.py:22
  456.9 196.1 %copy-start.5 = (f32[256,64]{0,1:T(8,128)S(1)}, f32[256,64]{0,1:T(8,128)}, u32[]{:S(2)}) copy-start(f32[256,64]{0,1:T(8,128)} %param.14) | copy-start | bytes 196612
  462.8 1.5 copy-start.8
  471.4 1.5 copy-start.8
  480.2 1.5 copy-start.8
  488.7 1.5 copy-start.8
  497.2 1.5 copy-start.8
  505.8 1.5 copy-start.8
  514.5 1.5 copy-start.8
  523.1 1.5 copy-start.8
  531.7 1.5 copy-start.8
  540.2 1.5 copy-start.8
  548.9 1.5 copy-start.8
  557.4 1.5 copy-start.8
  565.9 1.5 copy-start.8
  574.8 1.5 copy-start.8
  583.6 1.5 copy-start.8
  592.1 1.5 copy-start.8
  600.6 1.5 copy-start.8
  609.2 1.5 copy-start.8
  617.7 1.5 copy-start.8
  626.4 1.5 copy-start.8
  630.9 22.2 %collective-permute-start.17 = (f32[256,64]{0,1:T(8,128)S(1)}, f32[256,64]{0,1:T(8,128)S(1)}, u32[]{:S(2)}, u32[]{:S(2)}) collective-permute-start(f32[256,64]{0,1:T(8,128)S(1)} %fusion.50), channel_id=1, source_target_pairs={{0,8},{1,9},{2,10},{3,11},{4,12},{5,13},{6,14},{7,15},{8,0},{9,1},... | collective-permute-start | bytes 196616 | tf_op jit(solution)/shard_map/ppermute | solution.py:22
  653.7 0.7 copy-start.6
where the time goes:
time: 662 us; the launch traced here: 654 us
  waiting for transfers between devices  358 us (54%)
  starting transfers between devices  94.4 us (14%)
  matrix products  87.9 us (13%)
  local copies, waits for them, and re-layouts  85.6 us (13%)
  other arithmetic  25.3 us (4%)
    ppermute x18, waiting for transfers between devices, passed_along(): return lax.ppermute(value, axis, pairs)  358 us
    ppermute x18, starting transfers between devices, passed_along(): return lax.ppermute(value, axis, pairs)  94.4 us
    sub x20, matrix products, one_head(): shifted = jnp.where(mask_full, jnp.exp(scores - row_max), 0.0)  62.3 us
    another operation x20, local copies, waits for them, and re-layouts, one_head(): jnp.stack([part[row_local:row_local + 3, col_local:col_local + 3] for par...  47.8 us
    while x40, local copies, waits for them, and re-layouts  25.9 us
    dot_general x20, matrix products, one_head(): jnp.einsum('qtk,qkd->qtd', weights, value_tiles, preferred_element_type=j...  23.7 us
    concatenate x2, other arithmetic, direct_window(): planes.append(jnp.concatenate(row_parts, axis=0))  16.7 us
  transfers between devices with their start and end apart: 18, of which 6 were waited for; matrix products, arithmetic and copies ran while one was open for 2% of the time, Pallas kernels for 0%

commit v1 on v0

v1 whole, which is shorter than its diff:
```python
import functools
import math

import jax
import jax.numpy as jnp
from jax import lax
from jax.experimental import pallas as pl
from jax.experimental.pallas import tpu as pltpu
from jax.sharding import PartitionSpec as P

HEADS = 20
HD = 128
SH = 4
SW = 8
SAMPLE_STEPS = 50
GUIDANCE = 5.0
FLOW_SHIFT = 5.0

NT = (((1,), (1,)), ((), ()))
F32 = jnp.float32
BF16 = jnp.bfloat16

GR = SH // 2 + 1
GC = SW // 2 + 1
SLOTS = GR * GC


def flow_sigma(moment):
    remain = 1.0 - moment / SAMPLE_STEPS
    return FLOW_SHIFT * remain / (1.0 + (FLOW_SHIFT - 1.0) * remain)


def kernel(
    planes, tile_frames, tok, ch,
    q_hbm, k_hbm, v_hbm, mask_ref, wt_ref,
    out_ref,
    kwin, vwin, qwin, mwin, vloc, vsrc, wbuf, vel, vsib, vpart,
    k_sem, v_sem, q_sem, m_sem, x_sem,
    ks_send, vs_send, qs_send, m_send, x_send,
):
    half = q_hbm.shape[1] // 2
    pairs = half // (2 * HD)
    f = lax.axis_index("frame")
    c = f % 2
    pcol = f // 2 % 2
    prow = f // 4 % 2
    ft = f // 8 % tile_frames
    branch = f // (8 * tile_frames)
    sibling = f + 1 - 2 * c
    partner = f + 8 * tile_frames * (1 - 2 * branch)
    dvert = 4 - 8 * prow
    dhoriz = 2 - 4 * pcol
    base_even = f - c
    edge_u = 1 - prow
    edge_v = 1 - pcol
    own_base = 2 * (pcol * c + (1 - pcol) * (1 - c))
    sib_base = 2 - own_base
    steps = [0] + ([-1, 1] if planes == 3 else [])

    def plane_of(df):
        return df + 1 if planes == 3 else 0

    def exists(df):
        return jnp.logical_and(ft + df >= 0, ft + df < tile_frames)

    def guard(df, extra=None):
        conds = []
        if df != 0:
            conds.append(exists(df))
        if extra is not None:
            conds.append(extra)
        if not conds:
            return lambda fn: fn()
        return pl.when(functools.reduce(jnp.logical_and, conds))

    v_copy = pltpu.make_async_copy(v_hbm, vloc, x_sem.at[2])
    v_copy.start()

    def rel(u, i):
        ur = prow * u + (1 - prow) * (1 - u)
        v = pcol * i + (1 - pcol) * (1 - i)
        return ur, v

    local = []
    for u in range(2):
        for i in range(2):
            ur, v = rel(u, i)
            row = pl.multiple_of((u * 2 + v) * tok, tok)
            wr = own_base + i
            slot = (1 + ur) * GC + 1 + wr
            cols = pl.ds(pl.multiple_of(c * half, half), half)
            pltpu.make_async_copy(
                k_hbm.at[pl.ds(row, tok), cols],
                kwin.at[plane_of(0), slot], k_sem.at[plane_of(0), slot]).start()
            pltpu.make_async_copy(
                q_hbm.at[pl.ds(row, tok), cols],
                qwin.at[wr * 2 + ur], q_sem.at[wr * 2 + ur]).start()

    barrier = pltpu.get_barrier_semaphore()
    block = f - f % 8
    greeted = 0
    for df in steps:
        for other in range(8):
            target = block + 8 * df + other
            if df == 0:
                @pl.when(target != f)
                def _(target=target):
                    pl.semaphore_signal(barrier, inc=1, device_id={"frame": target},
                                        device_id_type=pl.DeviceIdType.MESH)
            else:
                @pl.when(exists(df))
                def _(target=target):
                    pl.semaphore_signal(barrier, inc=1, device_id={"frame": target},
                                        device_id_type=pl.DeviceIdType.MESH)
        if df == 0:
            greeted = 7
        else:
            greeted = greeted + 8 * exists(df).astype(jnp.int32)
    pl.semaphore_signal(barrier, inc=1, device_id={"frame": partner},
                        device_id_type=pl.DeviceIdType.MESH)
    pl.semaphore_wait(barrier, greeted + 1)

    sends = []
    number = 0
    edge_core = c == 1 - pcol
    for df in steps:
        there = plane_of(-df)
        for core in range(2):
            target = base_even + 8 * df + core + dvert
            for i in range(2):
                v = pcol * i + (1 - pcol) * (1 - i)
                sends.append((df, None, target, core, edge_u * 2 + v,
                              0 * GC + 1 + own_base + i, there))
        for core in range(2):
            target = base_even + 8 * df + core + dvert + dhoriz
            sends.append((df, edge_core, target, core, edge_u * 2 + edge_v, 0, there))
        for core in range(2):
            target = base_even + 8 * df + core + dhoriz
            for u in range(2):
                ur = prow * u + (1 - prow) * (1 - u)
                sends.append((df, edge_core, target, core, u * 2 + edge_v,
                              (1 + ur) * GC, there))
        for u in range(2):
            for i in range(2):
                ur, v = rel(u, i)
                slot = (1 + ur) * GC + 1 + own_base + i
                if df == 0:
                    sends.append((df, None, sibling, None, u * 2 + v, slot, there))
                else:
                    for core in range(2):
                        sends.append((df, None, base_even + 8 * df + core, core,
                                      u * 2 + v, slot, there))

    def k_copy(n):
        df, cond, target, core, tile, slot, there = sends[n]
        core = 1 - c if core is None else core
        return pltpu.make_async_remote_copy(
            src_ref=k_hbm.at[pl.ds(pl.multiple_of(tile * tok, tok), tok),
                             pl.ds(pl.multiple_of(core * half, half), half)],
            dst_ref=kwin.at[there, slot],
            send_sem=ks_send.at[n], recv_sem=k_sem.at[there, slot],
            device_id={"frame": target}, device_id_type=pl.DeviceIdType.MESH)

    def v_copy_out(n):
        df, cond, target, core, tile, slot, there = sends[n]
        core = 1 - c if core is None else core
        return pltpu.make_async_remote_copy(
            src_ref=vsrc.at[tile, core],
            dst_ref=vwin.at[there, slot],
            send_sem=vs_send.at[n], recv_sem=v_sem.at[there, slot],
            device_id={"frame": target}, device_id_type=pl.DeviceIdType.MESH)

    def each_send(make, act):
        for n, (df, cond, *_) in enumerate(sends):
            guard(df, cond)(lambda n=n: act(make(n)))

    each_send(k_copy, lambda copy: copy.start())

    def q_copy(u, i):
        ur, v = rel(u, i)
        place = (own_base + i) * 2 + ur
        return pltpu.make_async_remote_copy(
            src_ref=q_hbm.at[pl.ds(pl.multiple_of((u * 2 + v) * tok, tok), tok),
                             pl.ds(pl.multiple_of((1 - c) * half, half), half)],
            dst_ref=qwin.at[place],
            send_sem=qs_send.at[u * 2 + i], recv_sem=q_sem.at[place],
            device_id={"frame": sibling}, device_id_type=pl.DeviceIdType.MESH)

    for u in range(2):
        for i in range(2):
            q_copy(u, i).start()

    lane = lax.broadcasted_iota(jnp.int32, (1, 2 * tok), 1)
    for i in range(2):
        v = pcol * i + (1 - pcol) * (1 - i)
        for df in steps:
            for rr in range(GR):
                for dj in range(3):
                    col = pcol * dj + (1 - pcol) * (2 - dj)
                    row0 = prow * rr + (1 - prow) * (2 - rr)
                    first = mask_ref[edge_u * 2 + v, 9 * (df + 1) + 3 * row0 + col]
                    if rr > 0:
                        row1 = prow * (rr - 1) + (1 - prow) * (3 - rr)
                        second = mask_ref[prow * 2 + v, 9 * (df + 1) + 3 * row1 + col]
                    else:
                        second = 0
                    value = jnp.where(lane < tok, first, second)
                    if df != 0:
                        value = value * exists(df).astype(jnp.int32)
                    mwin[own_base + i, pl.ds((plane_of(df) * GR + rr) * 3 + dj, 1), :] = (
                        jnp.where(value > 0, 3e38, -1e30).astype(F32))
    m_copy = pltpu.make_async_remote_copy(
        src_ref=mwin.at[pl.ds(own_base, 2)], dst_ref=mwin.at[pl.ds(own_base, 2)],
        send_sem=m_send.at[0], recv_sem=m_sem.at[0],
        device_id={"frame": sibling}, device_id_type=pl.DeviceIdType.MESH)
    m_copy.start()

    v_copy.wait()

    def project(j, _):
        parts = []
        for e in range(2):
            cols = pl.ds(pl.multiple_of((2 * j + e) * HD, HD), HD)
            parts.append(lax.dot_general(wt_ref[:, cols], vloc[:, cols], NT,
                                         preferred_element_type=F32))
        side = j // pairs
        rows = pl.ds(pl.multiple_of((j % pairs) * ch, ch), ch)
        for t in range(4):
            both = jnp.concatenate(
                [part[:, t * tok:(t + 1) * tok] for part in parts], axis=1).astype(BF16)
            vsrc[t, side, rows, :] = both
        return 0

    lax.fori_loop(0, 2 * pairs, project, 0)
    each_send(v_copy_out, lambda copy: copy.start())
    for u in range(2):
        for i in range(2):
            ur, v = rel(u, i)
            slot = (1 + ur) * GC + 1 + own_base + i
            vwin[plane_of(0), slot] = vsrc[u * 2 + v, c]
    for df in steps[1:]:
        @pl.when(jnp.logical_not(exists(df)))
        def _(df=df):
            kwin[plane_of(df)] = jnp.zeros(kwin.shape[1:], kwin.dtype)
            vwin[plane_of(df)] = jnp.zeros(vwin.shape[1:], vwin.dtype)

    for place in range(8):
        pltpu.make_async_copy(qwin.at[place], qwin.at[place], q_sem.at[place]).wait()
    m_back = pltpu.make_async_remote_copy(
        src_ref=mwin.at[pl.ds(sib_base, 2)], dst_ref=mwin.at[pl.ds(sib_base, 2)],
        send_sem=m_send.at[0], recv_sem=m_sem.at[0],
        device_id={"frame": sibling}, device_id_type=pl.DeviceIdType.MESH)
    m_back.wait_recv()
    for df in steps:
        def arrive(df=df):
            p = plane_of(df)
            for slot in range(SLOTS):
                pltpu.make_async_copy(kwin.at[p, slot], kwin.at[p, slot],
                                      k_sem.at[p, slot]).wait()
        guard(df)(arrive)

    scale = math.log2(math.e) / math.sqrt(HD)

    def weigh(hp, _):
        for wr in range(4):
            ncol = min(3, GC - wr)
            for e in range(2):
                cols = pl.ds(pl.multiple_of((2 * hp + e) * HD, HD), HD)
                query = qwin[2 * wr:2 * wr + 2, :, cols].reshape(2 * tok, HD)
                blocks = []
                top = None
                for p in range(planes):
                    for rr in range(GR):
                        first = rr * GC + wr
                        keys = kwin[p, first:first + ncol, :, cols].reshape(ncol * tok, HD)
                        s = lax.dot_general(keys, query, NT, preferred_element_type=F32)
                        for dj in range(ncol):
                            line = (p * GR + rr) * 3 + dj
                            part = jnp.minimum(s[dj * tok:(dj + 1) * tok] * scale,
                                               mwin[wr, line:line + 1, :])
                            blocks.append(part)
                            here = jnp.max(part.reshape(tok // 8, 8, 2 * tok), axis=0)
                            top = here if top is None else jnp.maximum(top, here)
                top = jnp.max(top, axis=0, keepdims=True)
                total = None
                grown = []
                for part in blocks:
                    g = jnp.exp2(part - top)
                    grown.append(g)
                    here = jnp.sum(g.reshape(tok // 8, 8, 2 * tok), axis=0)
                    total = here if total is None else total + here
                inverse = 1.0 / jnp.sum(total, axis=0, keepdims=True)
                for n, g in enumerate(grown):
                    start = n * 2 * tok + e * tok
                    wbuf[hp, wr, start:start + tok, :] = (g * inverse).astype(BF16)
        return 0

    lax.fori_loop(0, pairs, weigh, 0)

    own_half_slots = own_base + 1
    for df in steps:
        def arrive(df=df):
            p = plane_of(df)
            for slot in range(SLOTS):
                copy = pltpu.make_async_copy(vwin.at[p, slot], vwin.at[p, slot], v_sem.at[p, slot])
                rr, cc = slot // GC, slot % GC
                if df == 0 and rr > 0 and cc > 0:
                    side = (cc - 1) // 2
                    pl.when(own_base != 2 * side)(lambda copy=copy: copy.wait())
                else:
                    copy.wait()
        guard(df)(arrive)

    def gather(hp, acc):
        rows = pl.ds(pl.multiple_of(hp * ch, ch), ch)
        result = []
        for wr in range(4):
            ncol = min(3, GC - wr)
            total = acc[wr]
            n = 0
            for p in range(planes):
                for rr in range(GR):
                    for dj in range(ncol):
                        slot = rr * GC + wr + dj
                        total = total + jnp.dot(
                            vwin[p, slot, rows, :],
                            wbuf[hp, wr, n * 2 * tok:(n + 1) * 2 * tok, :],
                            preferred_element_type=F32)
                        n += 1
            result.append(total)
        return tuple(result)

    acc = lax.fori_loop(0, pairs, gather,
                        tuple(jnp.zeros((ch, 2 * tok), F32) for _ in range(4)))
    for wr in range(4):
        vel[wr] = acc[wr]

    s_copy = pltpu.make_async_remote_copy(
        src_ref=vel.at[pl.ds(sib_base, 2)], dst_ref=vsib.at[0],
        send_sem=x_send.at[0], recv_sem=x_sem.at[0],
        device_id={"frame": sibling}, device_id_type=pl.DeviceIdType.MESH)
    s_copy.start()
    s_copy.wait_recv()
    mine = vel[pl.ds(own_base, 2)] + vsib[0]
    vsib[1] = mine
    p_copy = pltpu.make_async_remote_copy(
        src_ref=vsib.at[1], dst_ref=vpart,
        send_sem=x_send.at[1], recv_sem=x_sem.at[1],
        device_id={"frame": partner}, device_id_type=pl.DeviceIdType.MESH)
    p_copy.start()
    p_copy.wait_recv()
    other = vpart[...]
    is_cond = branch == 0
    cond = jnp.where(is_cond, mine, other)
    uncond = jnp.where(is_cond, other, mine)
    guided = uncond + GUIDANCE * (cond - uncond)
    for i in range(2):
        v = pcol * i + (1 - pcol) * (1 - i)
        turned = guided[i].T
        out_ref[pl.ds(pl.multiple_of((edge_u * 2 + v) * tok, tok), tok), :] = turned[:tok]
        out_ref[pl.ds(pl.multiple_of((prow * 2 + v) * tok, tok), tok), :] = turned[tok:]

    each_send(k_copy, lambda copy: copy.wait_send())
    each_send(v_copy_out, lambda copy: copy.wait_send())
    for u in range(2):
        for i in range(2):
            q_copy(u, i).wait_send()
    m_copy.wait_send()
    s_copy.wait_send()
    p_copy.wait_send()


def per_device(query_rows, key_rows, value_rows, tile_mask, head_weight, latent, step_index):
    frame_count = lax.axis_size("frame")
    tile_frames = frame_count // (2 * (SH // 2) * (SW // 2))
    planes = 3 if tile_frames > 1 else 1
    rows, width = query_rows.shape
    tok = rows // 4
    ch = head_weight.shape[1]
    half = width // 2
    pairs = half // (2 * HD)
    n_sends = 14 + (planes - 1) * 18
    lines = -(-planes * GR * 3 // 8) * 8
    dma = pltpu.SemaphoreType.DMA
    hbm = pl.BlockSpec(memory_space=pl.ANY)
    guided = pl.pallas_call(
        functools.partial(kernel, planes, tile_frames, tok, ch),
        out_shape=jax.ShapeDtypeStruct((rows, ch), F32),
        in_specs=[hbm, hbm, hbm, pl.BlockSpec(memory_space=pltpu.SMEM),
                  pl.BlockSpec(memory_space=pltpu.VMEM)],
        out_specs=pl.BlockSpec(memory_space=pltpu.VMEM),
        scratch_shapes=[
            pltpu.VMEM((planes, SLOTS, tok, half), BF16),
            pltpu.VMEM((planes, SLOTS, pairs * ch, 2 * tok), BF16),
            pltpu.VMEM((8, tok, half), BF16),
            pltpu.VMEM((4, lines, 2 * tok), F32),
            pltpu.VMEM((rows, width), BF16),
            pltpu.VMEM((4, 2, pairs * ch, 2 * tok), BF16),
            pltpu.VMEM((pairs, 4, planes * GR * 3 * 2 * tok, 2 * tok), BF16),
            pltpu.VMEM((4, ch, 2 * tok), F32),
            pltpu.VMEM((2, 2, ch, 2 * tok), F32),
            pltpu.VMEM((2, ch, 2 * tok), F32),
            dma((planes, SLOTS)), dma((planes, SLOTS)), dma((8,)), dma((1,)), dma((3,)),
            dma((n_sends,)), dma((n_sends,)), dma((4,)), dma((1,)), dma((2,)),
        ],
        compiler_params=pltpu.CompilerParams(
            collective_id=0, has_side_effects=True, vmem_limit_bytes=52 * 2**20),
    )(query_rows, key_rows, value_rows, tile_mask, head_weight.T)
    moment = step_index[0].astype(F32)
    sigma_now = flow_sigma(moment)
    step_size = flow_sigma(moment + 1.0) - sigma_now
    return guided, latent - sigma_now * guided, latent + step_size * guided


def solution(mesh):
    rows = P(("groups", "frame"), None)
    return jax.shard_map(
        per_device,
        mesh=mesh,
        in_specs=(rows, rows, rows, rows, P(), rows, P("groups")),
        out_specs=(rows, rows, rows),
        check_vma=False,
    )
```

time: 662 us -> 49.5 us (0.07); the launches traced: 654 us -> 49.3 us
  waiting for transfers between devices: 358 us -> 0 us
  starting transfers between devices: 94.4 us -> 0 us
  matrix products: 87.9 us -> 0 us
  local copies, waits for them, and re-layouts: 85.6 us -> 5.2 us
  Pallas kernels: 0 us -> 42.6 us
  other arithmetic: 25.3 us -> 0.03 us
    ppermute x18 -> x0, waiting for transfers between devices: 358 us -> none  [passed_along(): return lax.ppermute(value, axis, pairs)]
    ppermute x18 -> x0, starting transfers between devices: 94.4 us -> none  [passed_along(): return lax.ppermute(value, axis, pairs)]
    sub x20 -> x0, matrix products: 62.3 us -> none  [one_head(): shifted = jnp.where(mask_full, jnp.exp(scores - row_max), 0.0)]
    another operation x20 -> x0, local copies, waits for them, and re-layouts: 47.8 us -> none  [one_head(): jnp.stack([part[row_local:row_local + 3, col_local:col_local + 3] for par...]
    pallas_call x0 -> x1, Pallas kernels: none -> 42.6 us  [per_device(): pl.pallas_call(functools.partial(kernel, planes, tile_frames, tok, ch), o...]
    while x40 -> x0, local copies, waits for them, and re-layouts: 25.9 us -> none
    dot_general x21 -> x0, matrix products: 25.6 us -> none  [the longest x20 23.7 us: one_head(): jnp.einsum('qtk,qkd->qtd', weights, value_tiles, preferred_element_type=j...]
    concatenate x2 -> x0, other arithmetic: 16.7 us -> none  [direct_window(): planes.append(jnp.concatenate(row_parts, axis=0))]
  transfers between devices with their start and end apart: 18 -> 0, of which waited for: 6 -> 0; matrix products, arithmetic and copies ran while one was open for 2% -> 0% of each run, Pallas kernels for 0% -> 0%
where the time goes in v1:
time: 49.5 us; the launch traced here: 49.3 us
  Pallas kernels  42.6 us (86%)
  local copies, waits for them, and re-layouts  5.2 us (11%)
  between operations  1.4 us (3%)
    pallas_call x1, Pallas kernels, per_device(): pl.pallas_call(functools.partial(kernel, planes, tile_frames, tok, ch), o...  42.6 us
    unnamed x12, local copies, waits for them, and re-layouts  5.2 us

profile of v1, /device:TPU:0, one launch (start us, length us, event | category | flops | bytes accessed | tf_op | source)
XLA Modules:
  0.0 49.3 jit_solution(7188157444655440549)
XLA Ops:
  1.4 0.0 copy-start
  1.4 1.3 %copy-done = bf16[256,2560]{1,0:T(8,128)(2,1)S(1)} copy-done((bf16[256,2560]{1,0:T(8,128)(2,1)S(1)}, bf16[256,2560]{1,0:T(8,128)(2,1)}, u32[]{:S(2)}) %copy-start) | copy-done | bytes 1310744
  2.7 0.0 copy-start.1
  2.7 1.0 %copy-done.1 = bf16[2560,64]{0,1:T(8,128)(2,1)S(1)} copy-done((bf16[2560,64]{0,1:T(8,128)(2,1)S(1)}, bf16[2560,64]{0,1:T(8,128)(2,1)}, u32[]{:S(2)}) %copy-start.1) | copy-done | bytes 327704
  3.7 0.0 copy-start.2
  3.7 0.7 %copy-done.2 = s32[4,27]{1,0:T(4,128)S(1)} copy-done((s32[4,27]{1,0:T(4,128)S(1)}, s32[4,27]{1,0:T(4,128)}, u32[]{:S(2)}) %copy-start.2) | copy-done | bytes 456
  4.3 0.0 copy-start.3
  4.3 42.6 %shard_map.94 = f32[256,64]{1,0:T(8,128)S(1)} custom-call(bf16[256,2560]{1,0:T(8,128)(2,1)S(1)} %copy-done, bf16[256,2560]{1,0:T(8,128)(2,1)} %k_hbm.1, bf16[256,2560]{1,0:T(8,128)(2,1)} %v_hbm.1, s32[4,27]{1,0:T(4,128)S(1)} %copy-done.2, bf16[64,2560]{1,0:T(8,128)(2,1)S(1)} %bitcast.3), custom_call_target="tpu_custom_call" | custom-call | tf_op jit(solution)/shard_map/pallas_call | solution.py:386
  47.0 0.7 %copy.12 = f32[256,64]{0,1:T(8,128)} copy(f32[256,64]{1,0:T(8,128)S(1)} %shard_map.94) | data formatting | bytes 131072
  47.7 0.0 copy-done.3
  47.7 0.1 copy.10
  47.8 0.7 %copy.14 = f32[256,64]{0,1:T(8,128)} copy(f32[256,64]{1,0:T(8,128)S(1)} %get-tuple-element.6) | data formatting | bytes 131072
  48.6 0.7 %copy.13 = f32[256,64]{0,1:T(8,128)} copy(f32[256,64]{1,0:T(8,128)S(1)} %get-tuple-element.7) | data formatting | bytes 131072
  (1 shorter events, 0.0 us)
Async XLA Ops:
  1.4 1.3 %copy-start = (bf16[256,2560]{1,0:T(8,128)(2,1)S(1)}, bf16[256,2560]{1,0:T(8,128)(2,1)}, u32[]{:S(2)}) copy-start(bf16[256,2560]{1,0:T(8,128)(2,1)} %q_hbm.1) | copy-start | bytes 3932164
  2.7 1.0 %copy-start.1 = (bf16[2560,64]{0,1:T(8,128)(2,1)S(1)}, bf16[2560,64]{0,1:T(8,128)(2,1)}, u32[]{:S(2)}) copy-start(bf16[2560,64]{0,1:T(8,128)(2,1)} %param.11) | copy-start | bytes 983044
  3.7 0.7 %copy-start.2 = (s32[4,27]{1,0:T(4,128)S(1)}, s32[4,27]{1,0:T(4,128)}, u32[]{:S(2)}) copy-start(s32[4,27]{1,0:T(4,128)} %mask_ref.1) | copy-start | bytes 1300
  4.3 43.4 %copy-start.3 = (f32[256,64]{0,1:T(8,128)S(1)}, f32[256,64]{0,1:T(8,128)}, u32[]{:S(2)}) copy-start(f32[256,64]{0,1:T(8,128)} %param.12) | copy-start | bytes 196612

commit v2 on v1

--- a/solution.py
+++ b/solution.py
@@ -32,9 +32,9 @@
 
 def kernel(
     planes, tile_frames, tok, ch,
-    q_hbm, k_hbm, v_hbm, mask_ref, wt_ref,
+    q_hbm, k_hbm, v_hbm, mask_hbm, wt_hbm,
     out_ref,
-    kwin, vwin, qwin, mwin, vloc, vsrc, wbuf, vel, vsib, vpart,
+    mask_ref, wt_ref, kwin, vwin, qwin, mwin, vloc, vsrc, wbuf, vel, vsib, vpart,
     k_sem, v_sem, q_sem, m_sem, x_sem,
     ks_send, vs_send, qs_send, m_send, x_send,
 ):
@@ -75,6 +75,10 @@
 
     v_copy = pltpu.make_async_copy(v_hbm, vloc, x_sem.at[2])
     v_copy.start()
+    mask_copy = pltpu.make_async_copy(mask_hbm, mask_ref, x_sem.at[3])
+    mask_copy.start()
+    wt_copy = pltpu.make_async_copy(wt_hbm, wt_ref, x_sem.at[4])
+    wt_copy.start()
 
     def rel(u, i):
         ur = prow * u + (1 - prow) * (1 - u)
@@ -190,6 +194,7 @@
         for i in range(2):
             q_copy(u, i).start()
 
+    mask_copy.wait()
     lane = lax.broadcasted_iota(jnp.int32, (1, 2 * tok), 1)
     for i in range(2):
         v = pcol * i + (1 - pcol) * (1 - i)
@@ -216,6 +221,7 @@
     m_copy.start()
 
     v_copy.wait()
+    wt_copy.wait()
 
     def project(j, _):
         parts = []
@@ -349,16 +355,13 @@
         device_id={"frame": partner}, device_id_type=pl.DeviceIdType.MESH)
     p_copy.start()
     p_copy.wait_recv()
-    other = vpart[...]
-    is_cond = branch == 0
-    cond = jnp.where(is_cond, mine, other)
-    uncond = jnp.where(is_cond, other, mine)
-    guided = uncond + GUIDANCE * (cond - uncond)
-    for i in range(2):
-        v = pcol * i + (1 - pcol) * (1 - i)
-        turned = guided[i].T
-        out_ref[pl.ds(pl.multiple_of((edge_u * 2 + v) * tok, tok), tok), :] = turned[:tok]
-        out_ref[pl.ds(pl.multiple_of((prow * 2 + v) * tok, tok), tok), :] = turned[tok:]
+    left = lax.broadcasted_iota(jnp.int32, (ch, 2 * tok), 1) < tok
+    for place, held in ((branch, vsib.at[1]), (1 - branch, vpart)):
+        first, second = held[1 - pcol], held[pcol]
+        out_ref[place, :, pl.ds(pl.multiple_of(edge_u * 2 * tok, 2 * tok), 2 * tok)] = (
+            jnp.where(left, first, pltpu.roll(second, tok, 1)))
+        out_ref[place, :, pl.ds(pl.multiple_of(prow * 2 * tok, 2 * tok), 2 * tok)] = (
+            jnp.where(left, pltpu.roll(first, tok, 1), second))
 
     each_send(k_copy, lambda copy: copy.wait_send())
     each_send(v_copy_out, lambda copy: copy.wait_send())
@@ -382,14 +385,15 @@
     n_sends = 14 + (planes - 1) * 18
     lines = -(-planes * GR * 3 // 8) * 8
     dma = pltpu.SemaphoreType.DMA
-    hbm = pl.BlockSpec(memory_space=pl.ANY)
-    guided = pl.pallas_call(
+    hbm = pl.BlockSpec(memory_space=pltpu.HBM)
+    both = pl.pallas_call(
         functools.partial(kernel, planes, tile_frames, tok, ch),
-        out_shape=jax.ShapeDtypeStruct((rows, ch), F32),
-        in_specs=[hbm, hbm, hbm, pl.BlockSpec(memory_space=pltpu.SMEM),
-                  pl.BlockSpec(memory_space=pltpu.VMEM)],
+        out_shape=jax.ShapeDtypeStruct((2, ch, rows), F32),
+        in_specs=[hbm] * 5,
         out_specs=pl.BlockSpec(memory_space=pltpu.VMEM),
         scratch_shapes=[
+            pltpu.SMEM(tile_mask.shape, jnp.int32),
+            pltpu.VMEM((ch, width), BF16),
             pltpu.VMEM((planes, SLOTS, tok, half), BF16),
             pltpu.VMEM((planes, SLOTS, pairs * ch, 2 * tok), BF16),
             pltpu.VMEM((8, tok, half), BF16),
@@ -400,16 +404,18 @@
             pltpu.VMEM((4, ch, 2 * tok), F32),
             pltpu.VMEM((2, 2, ch, 2 * tok), F32),
             pltpu.VMEM((2, ch, 2 * tok), F32),
-            dma((planes, SLOTS)), dma((planes, SLOTS)), dma((8,)), dma((1,)), dma((3,)),
+            dma((planes, SLOTS)), dma((planes, SLOTS)), dma((8,)), dma((1,)), dma((5,)),
             dma((n_sends,)), dma((n_sends,)), dma((4,)), dma((1,)), dma((2,)),
         ],
         compiler_params=pltpu.CompilerParams(
-            collective_id=0, has_side_effects=True, vmem_limit_bytes=52 * 2**20),
+            collective_id=0, has_side_effects=True, vmem_limit_bytes=63 * 2**20),
     )(query_rows, key_rows, value_rows, tile_mask, head_weight.T)
     moment = step_index[0].astype(F32)
     sigma_now = flow_sigma(moment)
     step_size = flow_sigma(moment + 1.0) - sigma_now
-    return guided, latent - sigma_now * guided, latent + step_size * guided
+    guided = both[1] + GUIDANCE * (both[0] - both[1])
+    turned = latent.T
+    return guided.T, (turned - sigma_now * guided).T, (turned + step_size * guided).T
 
 
 def solution(mesh):

time: 49.5 us -> 45.8 us (0.925)
  local copies, waits for them, and re-layouts: 5.2 us -> 0.01 us
  other arithmetic: 0.03 us -> 1.57 us
    unnamed x12 -> x2, local copies, waits for them, and re-layouts: 5.2 us -> 0.01 us
    transpose x0 -> x1, other arithmetic: none -> 1.57 us  [per_device(): return (guided.T, (turned - sigma_now * guided).T, (turned + step_size *...]
where the time goes in v2:
time: 45.8 us; the launch traced here: 45.6 us
  Pallas kernels  42.6 us (93%)
  other arithmetic  1.57 us (3%)
  between operations  1.4 us (3%)
    pallas_call x1, Pallas kernels, per_device(): pl.pallas_call(functools.partial(kernel, planes, tile_frames, tok, ch), o...  42.6 us
    transpose x1, other arithmetic, per_device(): return (guided.T, (turned - sigma_now * guided).T, (turned + step_size *...  1.57 us

profile of v2, /device:TPU:0, one launch (start us, length us, event | category | flops | bytes accessed | tf_op | source)
XLA Modules:
  0.0 45.6 jit_solution(10055734601282219799)
XLA Ops:
  1.4 0.0 copy-start
  1.4 42.6 %shard_map.94 = f32[2,64,256]{2,1,0:T(8,128)} custom-call(bf16[256,2560]{1,0:T(8,128)(2,1)} %q_hbm.1, bf16[256,2560]{1,0:T(8,128)(2,1)} %k_hbm.1, bf16[256,2560]{1,0:T(8,128)(2,1)} %v_hbm.1, s32[4,27]{1,0:T(4,128)} %mask_hbm.1, bf16[64,2560]{1,0:T(8,128)(2,1)} %bitcast.36), custom_call_target="tpu_custom_call" | custom-call | tf_op jit(solution)/shard_map/pallas_call | solution.py:389
  44.0 0.0 copy-done
  44.0 1.6 %fusion.1 = (f32[256,64]{0,1:T(8,128)}, f32[256,64]{0,1:T(8,128)}, f32[256,64]{0,1:T(8,128)}) fusion(f32[256,64]{0,1:T(8,128)S(1)} %copy-done, f32[]{:T(128)S(6)} %sub.24, f32[2,64,256]{2,1,0:T(8,128)} %shard_map.94, f32[]{:T(128)} %bitcast.5), kind=kLoop, calls=%fused_computation.3 | loop fusion | flops 114688 | bytes 393224 | tf_op jit(solution)/shard_map/transpose | solution.py:418
Async XLA Ops:
  1.4 42.6 %copy-start = (f32[256,64]{0,1:T(8,128)S(1)}, f32[256,64]{0,1:T(8,128)}, u32[]{:S(2)}) copy-start(f32[256,64]{0,1:T(8,128)} %param.12) | copy-start | bytes 196612

commit v3 on v2

--- a/solution.py
+++ b/solution.py
@@ -34,9 +34,9 @@
     planes, tile_frames, tok, ch,
     q_hbm, k_hbm, v_hbm, mask_hbm, wt_hbm,
     out_ref,
-    mask_ref, wt_ref, kwin, vwin, qwin, mwin, vloc, vsrc, wbuf, vel, vsib, vpart,
+    mask_ref, wt_ref, kwin, vwin, qwin, mwin, vloc, vsrc, wbuf, vel, vsib, vsum, vpart,
     k_sem, v_sem, q_sem, m_sem, x_sem,
-    ks_send, vs_send, qs_send, m_send, x_send,
+    ks_send, vs_send, qs_send, m_send, x_send, f_send,
 ):
     half = q_hbm.shape[1] // 2
     pairs = half // (2 * HD)
@@ -55,6 +55,8 @@
     edge_v = 1 - pcol
     own_base = 2 * (pcol * c + (1 - pcol) * (1 - c))
     sib_base = 2 - own_base
+    own_group = own_base // 2
+    sib_group = 1 - own_group
     steps = [0] + ([-1, 1] if planes == 3 else [])
 
     def plane_of(df):
@@ -98,7 +100,7 @@
                 kwin.at[plane_of(0), slot], k_sem.at[plane_of(0), slot]).start()
             pltpu.make_async_copy(
                 q_hbm.at[pl.ds(row, tok), cols],
-                qwin.at[wr * 2 + ur], q_sem.at[wr * 2 + ur]).start()
+                qwin.at[ur * 4 + wr], q_sem.at[ur * 4 + wr]).start()
 
     barrier = pltpu.get_barrier_semaphore()
     block = f - f % 8
@@ -129,15 +131,12 @@
     edge_core = c == 1 - pcol
     for df in steps:
         there = plane_of(-df)
-        for core in range(2):
-            target = base_even + 8 * df + core + dvert
-            for i in range(2):
-                v = pcol * i + (1 - pcol) * (1 - i)
+        for i in range(2):
+            v = pcol * i + (1 - pcol) * (1 - i)
+            for core in range(2):
+                target = base_even + 8 * df + core + dvert
                 sends.append((df, None, target, core, edge_u * 2 + v,
-                              0 * GC + 1 + own_base + i, there))
-        for core in range(2):
-            target = base_even + 8 * df + core + dvert + dhoriz
-            sends.append((df, edge_core, target, core, edge_u * 2 + edge_v, 0, there))
+                              1 + own_base + i, there))
         for core in range(2):
             target = base_even + 8 * df + core + dhoriz
             for u in range(2):
@@ -182,7 +181,7 @@
 
     def q_copy(u, i):
         ur, v = rel(u, i)
-        place = (own_base + i) * 2 + ur
+        place = ur * 4 + own_base + i
         return pltpu.make_async_remote_copy(
             src_ref=q_hbm.at[pl.ds(pl.multiple_of((u * 2 + v) * tok, tok), tok),
                              pl.ds(pl.multiple_of((1 - c) * half, half), half)],
@@ -196,26 +195,31 @@
 
     mask_copy.wait()
     lane = lax.broadcasted_iota(jnp.int32, (1, 2 * tok), 1)
-    for i in range(2):
-        v = pcol * i + (1 - pcol) * (1 - i)
-        for df in steps:
-            for rr in range(GR):
-                for dj in range(3):
-                    col = pcol * dj + (1 - pcol) * (2 - dj)
-                    row0 = prow * rr + (1 - prow) * (2 - rr)
-                    first = mask_ref[edge_u * 2 + v, 9 * (df + 1) + 3 * row0 + col]
-                    if rr > 0:
-                        row1 = prow * (rr - 1) + (1 - prow) * (3 - rr)
-                        second = mask_ref[prow * 2 + v, 9 * (df + 1) + 3 * row1 + col]
-                    else:
-                        second = 0
-                    value = jnp.where(lane < tok, first, second)
+    for df in steps:
+        there = 9 * (df + 1)
+        for ur in range(2):
+            u = edge_u if ur == 0 else prow
+            for rr in range(ur, GR):
+                di = rr - ur
+                row = prow * di + (1 - prow) * (2 - di)
+                for k in range(4):
+                    sides = []
+                    for i in range(2):
+                        dj = k - i
+                        if 0 <= dj < 3:
+                            col = pcol * dj + (1 - pcol) * (2 - dj)
+                            v = pcol * i + (1 - pcol) * (1 - i)
+                            sides.append(mask_ref[u * 2 + v, there + 3 * row + col])
+                        else:
+                            sides.append(0)
+                    value = jnp.where(lane < tok, sides[0], sides[1])
                     if df != 0:
                         value = value * exists(df).astype(jnp.int32)
-                    mwin[own_base + i, pl.ds((plane_of(df) * GR + rr) * 3 + dj, 1), :] = (
+                    line = (ur * planes * GR + plane_of(df) * GR + rr) * 4 + k
+                    mwin[own_group, line:line + 1, :] = (
                         jnp.where(value > 0, 3e38, -1e30).astype(F32))
     m_copy = pltpu.make_async_remote_copy(
-        src_ref=mwin.at[pl.ds(own_base, 2)], dst_ref=mwin.at[pl.ds(own_base, 2)],
+        src_ref=mwin.at[own_group], dst_ref=mwin.at[own_group],
         send_sem=m_send.at[0], recv_sem=m_sem.at[0],
         device_id={"frame": sibling}, device_id_type=pl.DeviceIdType.MESH)
     m_copy.start()
@@ -250,118 +254,167 @@
             kwin[plane_of(df)] = jnp.zeros(kwin.shape[1:], kwin.dtype)
             vwin[plane_of(df)] = jnp.zeros(vwin.shape[1:], vwin.dtype)
 
-    for place in range(8):
-        pltpu.make_async_copy(qwin.at[place], qwin.at[place], q_sem.at[place]).wait()
-    m_back = pltpu.make_async_remote_copy(
-        src_ref=mwin.at[pl.ds(sib_base, 2)], dst_ref=mwin.at[pl.ds(sib_base, 2)],
-        send_sem=m_send.at[0], recv_sem=m_sem.at[0],
-        device_id={"frame": sibling}, device_id_type=pl.DeviceIdType.MESH)
-    m_back.wait_recv()
-    for df in steps:
-        def arrive(df=df):
+    def k_wait(slots):
+        for df in steps:
             p = plane_of(df)
-            for slot in range(SLOTS):
-                pltpu.make_async_copy(kwin.at[p, slot], kwin.at[p, slot],
-                                      k_sem.at[p, slot]).wait()
-        guard(df)(arrive)
+
+            def arrive(p=p):
+                for slot in slots:
+                    pltpu.make_async_copy(kwin.at[p, slot], kwin.at[p, slot],
+                                          k_sem.at[p, slot]).wait()
+            guard(df)(arrive)
+
+    def v_wait(slots):
+        for df in steps:
+            p = plane_of(df)
+
+            def arrive(p=p, df=df):
+                for slot in slots:
+                    copy = pltpu.make_async_copy(vwin.at[p, slot], vwin.at[p, slot],
+                                                 v_sem.at[p, slot])
+                    rr, cc = slot // GC, slot % GC
+                    if df == 0 and rr > 0 and cc > 0:
+                        side = (cc - 1) // 2
+                        pl.when(own_group != side)(lambda copy=copy: copy.wait())
+                    else:
+                        copy.wait()
+            guard(df)(arrive)
+
+    def forward(win, sem, kind, df):
+        p = plane_of(df)
+        return pltpu.make_async_remote_copy(
+            src_ref=win.at[p, 1], dst_ref=win.at[p, 0],
+            send_sem=f_send.at[p, kind], recv_sem=sem.at[p, 0],
+            device_id={"frame": f + dhoriz}, device_id_type=pl.DeviceIdType.MESH)
+
+    def hand_on(win, sem, kind):
+        for df in steps:
+            guard(df)(lambda df=df: forward(win, sem, kind, df).start())
+
+    inner_slots = list(range(GC, SLOTS))
+    outer_slots = list(range(2, GC)) + [0]
 
     scale = math.log2(math.e) / math.sqrt(HD)
 
-    def weigh(hp, _):
-        for wr in range(4):
-            ncol = min(3, GC - wr)
+    def weigh(ur, hp):
+        for group in range(2):
+            ncol = min(4, GC - 2 * group)
             for e in range(2):
                 cols = pl.ds(pl.multiple_of((2 * hp + e) * HD, HD), HD)
-                query = qwin[2 * wr:2 * wr + 2, :, cols].reshape(2 * tok, HD)
+                place = ur * 4 + 2 * group
+                query = qwin[place:place + 2, :, cols].reshape(2 * tok, HD)
                 blocks = []
                 top = None
                 for p in range(planes):
-                    for rr in range(GR):
-                        first = rr * GC + wr
+                    for rr in range(ur, GR):
+                        first = rr * GC + 2 * group
                         keys = kwin[p, first:first + ncol, :, cols].reshape(ncol * tok, HD)
                         s = lax.dot_general(keys, query, NT, preferred_element_type=F32)
-                        for dj in range(ncol):
-                            line = (p * GR + rr) * 3 + dj
-                            part = jnp.minimum(s[dj * tok:(dj + 1) * tok] * scale,
-                                               mwin[wr, line:line + 1, :])
-                            blocks.append(part)
+                        for k in range(ncol):
+                            line = (ur * planes * GR + p * GR + rr) * 4 + k
+                            part = jnp.minimum(s[k * tok:(k + 1) * tok] * scale,
+                                               mwin[group, line:line + 1, :])
+                            blocks.append(((p * GR + rr) * 4 + k, part))
                             here = jnp.max(part.reshape(tok // 8, 8, 2 * tok), axis=0)
                             top = here if top is None else jnp.maximum(top, here)
                 top = jnp.max(top, axis=0, keepdims=True)
                 total = None
                 grown = []
-                for part in blocks:
+                for n, part in blocks:
                     g = jnp.exp2(part - top)
-                    grown.append(g)
+                    grown.append((n, g))
                     here = jnp.sum(g.reshape(tok // 8, 8, 2 * tok), axis=0)
                     total = here if total is None else total + here
                 inverse = 1.0 / jnp.sum(total, axis=0, keepdims=True)
-                for n, g in enumerate(grown):
+                for n, g in grown:
                     start = n * 2 * tok + e * tok
-                    wbuf[hp, wr, start:start + tok, :] = (g * inverse).astype(BF16)
-        return 0
-
-    lax.fori_loop(0, pairs, weigh, 0)
-
-    own_half_slots = own_base + 1
-    for df in steps:
-        def arrive(df=df):
-            p = plane_of(df)
-            for slot in range(SLOTS):
-                copy = pltpu.make_async_copy(vwin.at[p, slot], vwin.at[p, slot], v_sem.at[p, slot])
-                rr, cc = slot // GC, slot % GC
-                if df == 0 and rr > 0 and cc > 0:
-                    side = (cc - 1) // 2
-                    pl.when(own_base != 2 * side)(lambda copy=copy: copy.wait())
-                else:
-                    copy.wait()
-        guard(df)(arrive)
-
-    def gather(hp, acc):
+                    wbuf[hp, group, start:start + tok, :] = (g * inverse).astype(BF16)
+
+    def gather(rows_of_grid, hp, acc):
         rows = pl.ds(pl.multiple_of(hp * ch, ch), ch)
         result = []
-        for wr in range(4):
-            ncol = min(3, GC - wr)
-            total = acc[wr]
-            n = 0
+        for group in range(2):
+            ncol = min(4, GC - 2 * group)
+            total = acc[group]
             for p in range(planes):
-                for rr in range(GR):
-                    for dj in range(ncol):
-                        slot = rr * GC + wr + dj
-                        total = total + jnp.dot(
-                            vwin[p, slot, rows, :],
-                            wbuf[hp, wr, n * 2 * tok:(n + 1) * 2 * tok, :],
-                            preferred_element_type=F32)
-                        n += 1
+                for rr in rows_of_grid:
+                    first = rr * GC + 2 * group
+                    n = (p * GR + rr) * 4
+                    values = jnp.concatenate(
+                        [vwin[p, first + k, rows, :] for k in range(ncol)], axis=1)
+                    total = total + jnp.dot(
+                        values, wbuf[hp, group, n * 2 * tok:(n + ncol) * 2 * tok, :],
+                        preferred_element_type=F32)
             result.append(total)
         return tuple(result)
 
-    acc = lax.fori_loop(0, pairs, gather,
-                        tuple(jnp.zeros((ch, 2 * tok), F32) for _ in range(4)))
-    for wr in range(4):
-        vel[wr] = acc[wr]
-
-    s_copy = pltpu.make_async_remote_copy(
-        src_ref=vel.at[pl.ds(sib_base, 2)], dst_ref=vsib.at[0],
-        send_sem=x_send.at[0], recv_sem=x_sem.at[0],
+    def weigh_all(ur):
+        def body(hp, _):
+            weigh(ur, hp)
+            return 0
+        lax.fori_loop(0, pairs, body, 0)
+
+    def gather_all(rows_of_grid, acc):
+        return lax.fori_loop(0, pairs, functools.partial(gather, rows_of_grid), acc)
+
+    nothing = tuple(jnp.zeros((ch, 2 * tok), F32) for _ in range(2))
+
+    def s_copy(ur):
+        return pltpu.make_async_remote_copy(
+            src_ref=vel.at[ur, sib_group], dst_ref=vsib.at[ur],
+            send_sem=x_send.at[ur], recv_sem=x_sem.at[ur],
+            device_id={"frame": sibling}, device_id_type=pl.DeviceIdType.MESH)
+
+    def p_copy(ur):
+        return pltpu.make_async_remote_copy(
+            src_ref=vsum.at[ur], dst_ref=vpart.at[ur],
+            send_sem=x_send.at[2 + ur], recv_sem=x_sem.at[5 + ur],
+            device_id={"frame": partner}, device_id_type=pl.DeviceIdType.MESH)
+
+    def give(ur, acc):
+        for group in range(2):
+            vel[ur, group] = acc[group]
+        s_copy(ur).start()
+
+    def pass_on(ur):
+        s_copy(ur).wait_recv()
+        vsum[ur] = vel[ur, own_group] + vsib[ur]
+        p_copy(ur).start()
+
+    def finish(ur):
+        p_copy(ur).wait_recv()
+        u = edge_u if ur == 0 else prow
+        lanes = pl.ds(pl.multiple_of(u * 2 * tok, 2 * tok), 2 * tok)
+        for place, held in ((branch, vsum), (1 - branch, vpart)):
+            value = held[ur]
+            out_ref[place, :, lanes] = jnp.where(
+                pcol == 1, value, pltpu.roll(value, tok, 1))
+
+    for place in range(8):
+        pltpu.make_async_copy(qwin.at[place], qwin.at[place], q_sem.at[place]).wait()
+    m_back = pltpu.make_async_remote_copy(
+        src_ref=mwin.at[sib_group], dst_ref=mwin.at[sib_group],
+        send_sem=m_send.at[0], recv_sem=m_sem.at[0],
         device_id={"frame": sibling}, device_id_type=pl.DeviceIdType.MESH)
-    s_copy.start()
-    s_copy.wait_recv()
-    mine = vel[pl.ds(own_base, 2)] + vsib[0]
-    vsib[1] = mine
-    p_copy = pltpu.make_async_remote_copy(
-        src_ref=vsib.at[1], dst_ref=vpart,
-        send_sem=x_send.at[1], recv_sem=x_sem.at[1],
-        device_id={"frame": partner}, device_id_type=pl.DeviceIdType.MESH)
-    p_copy.start()
-    p_copy.wait_recv()
-    left = lax.broadcasted_iota(jnp.int32, (ch, 2 * tok), 1) < tok
-    for place, held in ((branch, vsib.at[1]), (1 - branch, vpart)):
-        first, second = held[1 - pcol], held[pcol]
-        out_ref[place, :, pl.ds(pl.multiple_of(edge_u * 2 * tok, 2 * tok), 2 * tok)] = (
-            jnp.where(left, first, pltpu.roll(second, tok, 1)))
-        out_ref[place, :, pl.ds(pl.multiple_of(prow * 2 * tok, 2 * tok), 2 * tok)] = (
-            jnp.where(left, pltpu.roll(first, tok, 1), second))
+    m_back.wait_recv()
+    k_wait(inner_slots)
+    weigh_all(1)
+    k_wait([1])
+    hand_on(kwin, k_sem, 0)
+    v_wait(inner_slots)
+    give(1, gather_all(range(1, GR), nothing))
+    pass_on(1)
+
+    k_wait(outer_slots)
+    weigh_all(0)
+    v_wait([1])
+    hand_on(vwin, v_sem, 1)
+    acc = gather_all(range(1, GR), nothing)
+    finish(1)
+    v_wait(outer_slots)
+    give(0, gather_all(range(1), acc))
+    pass_on(0)
+    finish(0)
 
     each_send(k_copy, lambda copy: copy.wait_send())
     each_send(v_copy_out, lambda copy: copy.wait_send())
@@ -369,8 +422,14 @@
         for i in range(2):
             q_copy(u, i).wait_send()
     m_copy.wait_send()
-    s_copy.wait_send()
-    p_copy.wait_send()
+    for ur in range(2):
+        s_copy(ur).wait_send()
+        p_copy(ur).wait_send()
+    for df in steps:
+        def sent(df=df):
+            forward(kwin, k_sem, 0, df).wait_send()
+            forward(vwin, v_sem, 1, df).wait_send()
+        guard(df)(sent)
 
 
 def per_device(query_rows, key_rows, value_rows, tile_mask, head_weight, latent, step_index):
@@ -382,8 +441,8 @@
     ch = head_weight.shape[1]
     half = width // 2
     pairs = half // (2 * HD)
-    n_sends = 14 + (planes - 1) * 18
-    lines = -(-planes * GR * 3 // 8) * 8
+    n_sends = 12 + (planes - 1) * 16
+    lines = -(-2 * planes * GR * 4 // 8) * 8
     dma = pltpu.SemaphoreType.DMA
     hbm = pl.BlockSpec(memory_space=pltpu.HBM)
     both = pl.pallas_call(
@@ -397,15 +456,16 @@
             pltpu.VMEM((planes, SLOTS, tok, half), BF16),
             pltpu.VMEM((planes, SLOTS, pairs * ch, 2 * tok), BF16),
             pltpu.VMEM((8, tok, half), BF16),
-            pltpu.VMEM((4, lines, 2 * tok), F32),
+            pltpu.VMEM((2, lines, 2 * tok), F32),
             pltpu.VMEM((rows, width), BF16),
             pltpu.VMEM((4, 2, pairs * ch, 2 * tok), BF16),
-            pltpu.VMEM((pairs, 4, planes * GR * 3 * 2 * tok, 2 * tok), BF16),
-            pltpu.VMEM((4, ch, 2 * tok), F32),
+            pltpu.VMEM((pairs, 2, planes * GR * 4 * 2 * tok, 2 * tok), BF16),
             pltpu.VMEM((2, 2, ch, 2 * tok), F32),
             pltpu.VMEM((2, ch, 2 * tok), F32),
-            dma((planes, SLOTS)), dma((planes, SLOTS)), dma((8,)), dma((1,)), dma((5,)),
-            dma((n_sends,)), dma((n_sends,)), dma((4,)), dma((1,)), dma((2,)),
+            pltpu.VMEM((2, ch, 2 * tok), F32),
+            pltpu.VMEM((2, ch, 2 * tok), F32),
+            dma((planes, SLOTS)), dma((planes, SLOTS)), dma((8,)), dma((1,)), dma((7,)),
+            dma((n_sends,)), dma((n_sends,)), dma((4,)), dma((1,)), dma((4,)), dma((planes, 2)),
         ],
         compiler_params=pltpu.CompilerParams(
             collective_id=0, has_side_effects=True, vmem_limit_bytes=63 * 2**20),

time: 45.8 us -> 38.5 us (0.84)
  Pallas kernels: 42.6 us -> 35.3 us
    pallas_call x1, Pallas kernels: 42.6 us -> 35.3 us  [per_device(): pl.pallas_call(functools.partial(kernel, planes, tile_frames, tok, ch), o...]
where the time goes in v3:
time: 38.5 us; the launch traced here: 38.3 us
  Pallas kernels  35.3 us (92%)
  other arithmetic  1.57 us (4%)
  between operations  1.4 us (4%)
    pallas_call x1, Pallas kernels, per_device(): pl.pallas_call(functools.partial(kernel, planes, tile_frames, tok, ch), o...  35.3 us
    transpose x1, other arithmetic, per_device(): return (guided.T, (turned - sigma_now * guided).T, (turned + step_size *...  1.57 us

profile of v3, /device:TPU:0, one launch (start us, length us, event | category | flops | bytes accessed | tf_op | source)
XLA Modules:
  0.0 38.3 jit_solution(9168004272720975840)
XLA Ops:
  1.4 0.0 copy-start
  1.4 35.3 %shard_map.94 = f32[2,64,256]{2,1,0:T(8,128)} custom-call(bf16[256,2560]{1,0:T(8,128)(2,1)} %q_hbm.1, bf16[256,2560]{1,0:T(8,128)(2,1)} %k_hbm.1, bf16[256,2560]{1,0:T(8,128)(2,1)} %v_hbm.1, s32[4,27]{1,0:T(4,128)} %mask_hbm.1, bf16[64,2560]{1,0:T(8,128)(2,1)} %bitcast.36), custom_call_target="tpu_custom_call" | custom-call | tf_op jit(solution)/shard_map/pallas_call | solution.py:448
  36.7 0.0 copy-done
  36.7 1.6 %fusion.1 = (f32[256,64]{0,1:T(8,128)}, f32[256,64]{0,1:T(8,128)}, f32[256,64]{0,1:T(8,128)}) fusion(f32[256,64]{0,1:T(8,128)S(1)} %copy-done, f32[]{:T(128)S(6)} %sub.24, f32[2,64,256]{2,1,0:T(8,128)} %shard_map.94, f32[]{:T(128)} %bitcast.5), kind=kLoop, calls=%fused_computation.3 | loop fusion | flops 114688 | bytes 393224 | tf_op jit(solution)/shard_map/transpose | solution.py:478
Async XLA Ops:
  1.4 35.4 %copy-start = (f32[256,64]{0,1:T(8,128)S(1)}, f32[256,64]{0,1:T(8,128)}, u32[]{:S(2)}) copy-start(f32[256,64]{0,1:T(8,128)} %param.12) | copy-start | bytes 196612
